TPU v7x, 32 devices: a whole 2x2x4 slice. The times are simulated.
32 devices in a mesh: kpt: 2 (over x), col: 16 (over z, y, core).
Axes of the slice: x: 2, y: 2, z: 4, core: 2. Of those that a mesh axis runs over, the one named last changes fastest.
Arguments:
- ancestor_rows: bfloat16 [4, 1024, 1024], P('kpt', 'col'), parts along dimension 0, may hold values from -0.375 to 0.375
- factor_rows: bfloat16 [80, 4, 64, 256], P('col', 'kpt'), parts along dimension 1, may hold values from -1.5 to 1.5
- pattern: int32 [80, 4], P('col'), may hold values from 0 to 15, as said below
- lengths: int32 [80], P('col'), may hold values from 2 to 4, as said below
- diag_inverse: float32 [80, 128, 128], P('col', 'kpt'), parts along dimension 1, may hold values from -6 to 6
- pole_weight: float32 [2], replicated, may hold values from 0.5 to 2
Outputs:
- inverse_row: bfloat16 [80, 4, 64, 256], P('col', 'kpt'), parts along dimension 1
- inverse_diag: float32 [80, 128, 128], P('col', 'kpt'), parts along dimension 1
- density: bfloat16 [80, 128, 256], P('col', 'kpt'), parts along dimension 1
There are 2 independent parts, one for each index of `kpt`. A program takes and returns all parts, laid end to end along the dimension named above; an argument that names none is the same for every part. Nothing has to cross between parts.
Inputs may be any that keep to these rules, and one draw needn't show every extreme that they name: `pattern`: row k lists the ancestors of supernode k's structure; entries at positions lengths[k] or later are not used. The used entries of one row are distinct. Over the 5 supernodes of one device (aligned blocks of 5 rows), one ancestor is named by at most 2 used entries. `lengths`: the first supernode of each device's aligned block of 5 rows has 4 blocks.
All inputs are finite; a program needn't handle non-finite values.
Results may differ from a plain program's by a relative error of at most 0.0051.
Values may be sent and summed in bfloat16 or wider, within the bound.
A program may use at most 192 MiB of HBM per device.

v0:
```python
import jax
import jax.numpy as jnp
from jax import lax
from jax.sharding import PartitionSpec as P

CAP = 2


def slot_layout(pattern, lengths, devices_total, capacity):
    supernodes, blocks = pattern.shape
    live_slots = jnp.arange(blocks)[None, :] < lengths[:, None]
    targets = pattern.reshape(-1)
    live_flat = live_slots.reshape(-1)
    pair_total = supernodes * blocks
    positions = jnp.arange(pair_total)
    earlier = (
        (targets[:, None] == targets[None, :])
        & live_flat[None, :]
        & (positions[None, :] < positions[:, None])
    )
    ranking = jnp.sum(earlier, axis=1)
    slot_total = devices_total * capacity
    slot_of_pair = jnp.where(live_flat, targets * capacity + ranking, slot_total)
    matches = jnp.arange(slot_total)[:, None] == slot_of_pair[None, :]
    source_pair = jnp.sum(jnp.where(matches, positions[None, :], 0), axis=1)
    occupied = jnp.any(matches, axis=1)
    return (live_slots, live_flat, slot_of_pair, source_pair // blocks, occupied)


def shards(ancestor_rows, factor_rows, pattern, lengths, diag_inverse, pole_weight):
    supernodes, pole_count, block_width, row_span = factor_rows.shape
    blocks = pattern.shape[1]
    devices_total = lax.axis_size("col")
    capacity = CAP
    slot_total = devices_total * capacity
    live_slots, live_flat, slot_of_pair, source_super, occupied = slot_layout(
        pattern, lengths, devices_total, capacity
    )
    live_columns = jnp.repeat(live_slots, block_width, axis=1).astype(jnp.bfloat16)
    masked_factor = factor_rows * live_columns[:, None, None, :]
    ancestors = ancestor_rows.shape[2] // block_width
    request = jnp.where(occupied[:, None], jnp.take(pattern, source_super, axis=0), 0)
    request = request.reshape(devices_total, capacity, blocks)
    clipped = jnp.minimum(slot_of_pair, slot_total - 1)
    table = ancestor_rows.reshape(pole_count, block_width, ancestors, block_width)
    outgoing = jnp.take(masked_factor, source_super, axis=0)
    outgoing = outgoing.reshape(devices_total, capacity, pole_count, block_width, row_span)
    factor_part = lax.all_to_all(outgoing, "col", split_axis=0, concat_axis=0, tiled=True)
    indices = lax.all_to_all(request, "col", split_axis=0, concat_axis=0, tiled=True)
    peer_count = indices.shape[0]
    slot_depth = indices.shape[1]
    gathered = jnp.take(table, indices, axis=2)
    gathered = gathered.reshape(
        pole_count, block_width, peer_count, slot_depth, blocks * block_width
    )
    products = jnp.einsum(
        "ncpix,pjncx->ncipj", factor_part, gathered, preferred_element_type=jnp.float32
    )
    rounded = products.astype(jnp.bfloat16).reshape(
        peer_count, slot_depth, block_width, pole_count * block_width
    )
    returned = lax.all_to_all(rounded, "col", split_axis=0, concat_axis=0, tiled=True)
    per_pair = jnp.take(
        returned.reshape(slot_total, block_width, pole_count, block_width), clipped, axis=0
    )
    per_pair = per_pair * live_flat.astype(jnp.bfloat16)[:, None, None, None]
    column_blocks = jnp.transpose(
        per_pair.reshape(supernodes, blocks, block_width, pole_count, block_width), (0, 3, 2, 1, 4)
    )
    column_blocks = column_blocks.reshape(supernodes, pole_count, block_width, row_span)
    inverse_row = -column_blocks
    diagonal = jnp.einsum(
        "kpic,kpjc->kipj", masked_factor, column_blocks, preferred_element_type=jnp.float32
    )
    inverse_diag = diag_inverse + diagonal.reshape(
        supernodes, block_width, pole_count * block_width
    )
    density = -jnp.sum(pole_weight[None, :, None, None] * column_blocks.astype(jnp.float32), axis=1)
    return (inverse_row, inverse_diag, density.astype(jnp.bfloat16))


def solution(mesh):
    placed = (
        P("kpt", "col", None),
        P("col", "kpt", None, None),
        P("col", None),
        P("col"),
        P("col", "kpt", None),
        P(),
    )
    return jax.shard_map(
        shards,
        mesh=mesh,
        in_specs=placed,
        out_specs=(P("col", "kpt", None, None), P("col", "kpt", None), P("col", "kpt", None)),
        check_vma=False,
    )
```

profile of v0, /device:TPU:1, one launch (start us, length us, event | category | flops | bytes accessed | tf_op | source)
XLA Modules:
  0.0 98.3 jit_solution(7906934559234065477)
XLA Ops:
  0.6 0.8 copy.64
  1.5 0.7 iota_compare_fusion.2
  2.3 0.2 convert_reduce_fusion
  2.8 0.6 gather_fusion
  3.5 0.7 select_select_fusion
  4.2 7.3 %all-to-all-start = ((s32[16,2,4]{2,1,0:T(2,128)}), s32[16,2,4]{2,1,0:T(2,128)S(1)}, u32[]{:S(2)}, u32[]{:S(2)}) async-start(s32[16,2,4]{2,1,0:T(2,128)} %select_select_fusion), calls=%async_computation | async-start | bytes 32768 | tf_op jit(solution)/shard_map/all_to_all | solution.py:49
  11.6 0.7 compare_and_fusion.2
  12.5 1.0 %broadcast_multiply_fusion = bf16[5,2,64,256]{3,2,1,0:T(8,128)(2,1)S(1)} fusion(bf16[5,2,64,256]{3,2,1,0:T(8,128)(2,1)} %param.7, bf16[5,256]{1,0:T(8,128)(2,1)S(1)} %convert_element_type.37), kind=kLoop, calls=%fused_computation.13 | loop fusion | flops 163840 | bytes 657920 | tf_op jit(solution)/shard_map/mul | solution.py:40
  13.5 0.7 gather_fusion.2
  14.2 1.6 %broadcast_select_fusion = bf16[16,2,2,64,256]{4,3,2,1,0:T(8,128)(2,1)} fusion(bf16[16,2,2,64,256]{4,3,2,1,0:T(8,128)(2,1)S(1)} %bitcast.47, pred[16,2]{1,0:T(8,128)(4,1)S(1)} %compare_and_fusion.1), kind=kLoop, calls=%fused_computation.6 | loop fusion | flops 1048576 | bytes 4194336 | tf_op jit(solution)/shard_map/jit(_take)/select_n | solution.py:46
  15.8 1.6 %all-to-all-done = s32[16,2,4]{2,1,0:T(2,128)S(1)} async-done(((s32[16,2,4]{2,1,0:T(2,128)}), s32[16,2,4]{2,1,0:T(2,128)S(1)}, u32[]{:S(2)}, u32[]{:S(2)}) %all-to-all-start) | async-done | bytes 544 | tf_op jit(solution)/shard_map/all_to_all | solution.py:49
  17.4 4.9 %all-to-all-start.1 = ((bf16[16,2,2,64,256]{4,3,2,1,0:T(8,128)(2,1)}), bf16[16,2,2,64,256]{4,3,2,1,0:T(8,128)(2,1)}, u32[]{:S(2)}, u32[]{:S(2)}) async-start(bf16[16,2,2,64,256]{4,3,2,1,0:T(8,128)(2,1)} %broadcast_select_fusion), calls=%async_computation.1 | async-start | bytes 4194304 | tf_op jit(solution)/shard_map/all_to_all | solution.py:48
  22.3 0.3 reshape.235
  22.9 3.0 %gather_fusion.1 = bf16[128,2,64,64]{3,2,1,0:T(8,128)(2,1)} fusion(bf16[2,64,16,64]{3,1,2,0:T(8,128)(2,1)S(1)} %copy.69, s32[1024]{0:T(1024)S(1)} %pad_clamp_fusion.1), kind=kCustom, calls=%fused_computation.1 | custom fusion | bytes 4194816 | tf_op jit(solution)/shard_map/jit(_take)/gather | solution.py:52
  26.0 12.5 %copy.70 = bf16[2,64,16,2,4,64]{5,4,1,0,3,2:T(4,128)(2,1)} copy(bf16[2,64,16,2,4,64]{5,1,0,4,3,2:T(8,128)(2,1)} %bitcast.46) | data formatting | bytes 4194304 | tf_op jit(solution)/shard_map/jit(_take)/gather | solution.py:52
  38.5 6.1 %gather.27 = bf16[2,64,16,2,256]{4,1,0,3,2:T(8,128)(2,1)S(1)} reshape(bf16[2,64,16,2,4,64]{5,4,1,0,3,2:T(4,128)(2,1)} %copy.70) | data formatting | bytes 4194304 | tf_op jit(solution)/shard_map/jit(_take)/gather | solution.py:52
  44.9 19.0 %all-to-all-done.1 = bf16[16,2,2,64,256]{4,3,2,1,0:T(8,128)(2,1)} async-done(((bf16[16,2,2,64,256]{4,3,2,1,0:T(8,128)(2,1)}), bf16[16,2,2,64,256]{4,3,2,1,0:T(8,128)(2,1)}, u32[]{:S(2)}, u32[]{:S(2)}) %all-to-all-start.1) | async-done | bytes 2097184 | tf_op jit(solution)/shard_map/all_to_all | solution.py:48
  63.9 2.3 %fusion.3 = bf16[16,2,2,64,64]{4,3,2,1,0:T(8,128)(2,1)S(1)} fusion(bf16[16,2,2,64,256]{4,3,2,1,0:T(8,128)(2,1)} %all-to-all-done.1, bf16[2,64,16,2,256]{4,1,0,3,2:T(8,128)(2,1)S(1)} %gather.27, pred[16,2,256]{2,1,0:T(4,128)(4,1)S(1)} %copy.68), kind=kOutput, calls=%fused_computation.8 | convolution fusion | flops 135528448 | bytes 4726784 | tf_op jit(solution)/shard_map/ncpix,pjncx->ncipj/dot_general | solution.py:56
  66.2 1.1 %copy.71 = bf16[16,2,64,128]{3,2,1,0:T(8,128)(2,1)} copy(bf16[16,2,64,128]{2,3,1,0:T(8,128)(2,1)S(1)} %bitcast.50) | data formatting | bytes 1048576 | tf_op jit(solution)/shard_map/reshape | solution.py:59
  67.3 10.8 %all-to-all-start.2 = ((bf16[16,2,64,128]{3,2,1,0:T(8,128)(2,1)}), bf16[16,2,64,128]{3,2,1,0:T(8,128)(2,1)S(1)}, u32[]{:S(2)}, u32[]{:S(2)}) async-start(bf16[16,2,64,128]{3,2,1,0:T(8,128)(2,1)} %copy.71), calls=%async_computation.2 | async-start | bytes 1048576 | tf_op jit(solution)/shard_map/all_to_all | solution.py:62
  78.4 13.9 %all-to-all-done.2 = bf16[16,2,64,128]{3,2,1,0:T(8,128)(2,1)S(1)} async-done(((bf16[16,2,64,128]{3,2,1,0:T(8,128)(2,1)}), bf16[16,2,64,128]{3,2,1,0:T(8,128)(2,1)S(1)}, u32[]{:S(2)}, u32[]{:S(2)}) %all-to-all-start.2) | async-done | bytes 524320 | tf_op jit(solution)/shard_map/all_to_all | solution.py:62
  92.3 0.4 reshape.237
  92.7 0.3 copy.72
  92.9 0.7 gather_fusion.3
  93.6 0.6 multiply_reduce_fusion
  94.2 0.5 copy.73
  94.8 0.4 reshape.238
  95.2 0.2 fusion.17
  95.4 0.8 neg.7
  96.5 0.3 copy.75
  96.7 0.9 convert_element_type.42
  97.6 0.7 add.96
  (35 shorter events, 1.7 us)
Async XLA Ops:
  4.2 13.2 %all-to-all-start = ((s32[16,2,4]{2,1,0:T(2,128)}), s32[16,2,4]{2,1,0:T(2,128)S(1)}, u32[]{:S(2)}, u32[]{:S(2)}) async-start(s32[16,2,4]{2,1,0:T(2,128)} %select_select_fusion), calls=%async_computation | async-start | bytes 32768 | tf_op jit(solution)/shard_map/all_to_all | solution.py:49
  15.8 6.5 %copy-start = (bf16[2,64,1024]{2,1,0:T(8,128)(2,1)S(1)}, bf16[2,64,1024]{2,1,0:T(8,128)(2,1)}, u32[]{:S(2)}) copy-start(bf16[2,64,1024]{2,1,0:T(8,128)(2,1)} %param.6) | copy-start | bytes 786436
  17.4 46.5 %all-to-all-start.1 = ((bf16[16,2,2,64,256]{4,3,2,1,0:T(8,128)(2,1)}), bf16[16,2,2,64,256]{4,3,2,1,0:T(8,128)(2,1)}, u32[]{:S(2)}, u32[]{:S(2)}) async-start(bf16[16,2,2,64,256]{4,3,2,1,0:T(8,128)(2,1)} %broadcast_select_fusion), calls=%async_computation.1 | async-start | bytes 4194304 | tf_op jit(solution)/shard_map/all_to_all | solution.py:48
  67.3 24.9 %all-to-all-start.2 = ((bf16[16,2,64,128]{3,2,1,0:T(8,128)(2,1)}), bf16[16,2,64,128]{3,2,1,0:T(8,128)(2,1)S(1)}, u32[]{:S(2)}, u32[]{:S(2)}) async-start(bf16[16,2,64,128]{3,2,1,0:T(8,128)(2,1)} %copy.71), calls=%async_computation.2 | async-start | bytes 1048576 | tf_op jit(solution)/shard_map/all_to_all | solution.py:62
  92.7 1.0 copy-start.2
  95.2 2.4 %copy-start.1 = (f32[5,64,128]{2,1,0:T(8,128)S(1)}, f32[5,64,128]{2,1,0:T(8,128)}, u32[]{:S(2)}) copy-start(f32[5,64,128]{2,1,0:T(8,128)} %param.10) | copy-start | bytes 491524
where the time goes:
time: 99.3 us; the launch traced here: 98.3 us
  waiting for transfers between devices  34.5 us (35%)
  local copies, waits for them, and re-layouts  30 us (30%)
  starting transfers between devices  23.1 us (23%)
  other arithmetic  7.35 us (7%)
  matrix products  2.51 us (3%)
    gather x3, local copies, waits for them, and re-layouts, shards(): gathered = jnp.take(table, indices, axis=2)  21.7 us
    all_to_all x1, waiting for transfers between devices, shards(): lax.all_to_all(outgoing, 'col', split_axis=0, concat_axis=0, tiled=True)  19 us
    all_to_all x1, waiting for transfers between devices, shards(): lax.all_to_all(rounded, 'col', split_axis=0, concat_axis=0, tiled=True)  13.9 us
    all_to_all x1, starting transfers between devices, shards(): lax.all_to_all(rounded, 'col', split_axis=0, concat_axis=0, tiled=True)  10.8 us
    all_to_all x1, starting transfers between devices, shards(): lax.all_to_all(request, 'col', split_axis=0, concat_axis=0, tiled=True)  7.35 us
    all_to_all x1, starting transfers between devices, shards(): lax.all_to_all(outgoing, 'col', split_axis=0, concat_axis=0, tiled=True)  4.92 us
    dot_general x1, matrix products, shards(): jnp.einsum('ncpix,pjncx->ncipj', factor_part, gathered, preferred_element...  2.28 us
  transfers between devices with their start and end apart: 3, of which 3 were waited for; matrix products, arithmetic and copies ran while one was open for 27% of the time, Pallas kernels for 0%

commit v1 on v0

--- a/solution.py
+++ b/solution.py
@@ -1,9 +1,226 @@
+import functools
+
 import jax
 import jax.numpy as jnp
 from jax import lax
+from jax.experimental import pallas as pl
+from jax.experimental.pallas import tpu as pltpu
 from jax.sharding import PartitionSpec as P
 
 CAP = 2
+MESH = pl.DeviceIdType.MESH
+TABLE_BYTES = 16 * 2**20
+VMEM_BYTES = 32 * 2**20
+LEFT, RIGHT, ACROSS, TWIN = range(4)
+
+
+def gather_kernel(
+    line, lag,
+    pattern, lengths, weight, anc, factor_hbm, diag_hbm,
+    row_out, diag_out, density_out,
+    *scratch,
+):
+    poles, width, span = anc.shape
+    tables = scratch[:poles]
+    factor, diag, spread, partial, send_sem, recv_sem, local_sem = scratch[poles:]
+    supernodes = factor.shape[0]
+    blocks = pattern.shape[1]
+    me = lax.axis_index("col")
+    core, row, z = me % 2, (me // 2) % 2, me // 4
+
+    def index(at_z, at_row, at_core):
+        return (at_z * 2 + at_row) * 2 + at_core
+
+    targets = {
+        LEFT: index(z - 1, row, core),
+        RIGHT: index(z + 1, row, core),
+        ACROSS: index(z, 1 - row, core),
+        TWIN: index(z, row, 1 - core),
+    }
+    has = {LEFT: z > 0, RIGHT: z < line - 1}
+
+    factor_in = pltpu.make_async_copy(factor_hbm, factor, local_sem.at[0])
+    diag_in = pltpu.make_async_copy(diag_hbm, diag, local_sem.at[1])
+    factor_in.start()
+    diag_in.start()
+    for p in range(poles):
+        for strip in range(span // (2 * width)):
+            tables[p][me, strip] = anc[p, :, strip * 2 * width:(strip + 1) * 2 * width]
+
+    barrier = pltpu.get_barrier_semaphore()
+
+    def greet(way):
+        pl.semaphore_signal(barrier, inc=1, device_id={"col": targets[way]}, device_id_type=MESH)
+
+    greet(TWIN)
+    greet(ACROSS)
+    for way in (LEFT, RIGHT):
+        pl.when(has[way])(functools.partial(greet, way))
+    pl.semaphore_wait(barrier, 2 + has[LEFT].astype(jnp.int32) + has[RIGHT].astype(jnp.int32))
+
+    def remote(way, origin, p, source):
+        return pltpu.make_async_remote_copy(
+            src_ref=source,
+            dst_ref=tables[p].at[origin],
+            send_sem=send_sem.at[way, origin, p],
+            recv_sem=recv_sem.at[origin, p],
+            device_id={"col": targets[way]},
+            device_id_type=MESH,
+        )
+
+    def send(way, origin, p, source):
+        remote(way, origin, p, source).start()
+
+    def arrived(origin, p):
+        remote(TWIN, origin, p, tables[p].at[origin]).wait_recv()
+
+    def own(p):
+        block = tables[p].at[me]
+        for way in (LEFT, RIGHT):
+            pl.when(has[way])(functools.partial(send, way, me, p, block))
+        send(ACROSS, me, p, block)
+        send(TWIN, me, p, block)
+
+    def from_line(p, side, distance):
+        at_z = z - distance if side == LEFT else z + distance
+        inside = at_z >= 0 if side == LEFT else at_z < line
+        onward = RIGHT if side == LEFT else LEFT
+
+        @pl.when(inside)
+        def _():
+            origin = index(at_z, row, core)
+            arrived(origin, p)
+            block = tables[p].at[origin]
+            pl.when(has[onward])(functools.partial(send, onward, origin, p, block))
+            send(ACROSS, origin, p, block)
+            send(TWIN, origin, p, block)
+
+    def from_across(p, distance):
+        for sign in (-1, 1) if distance else (1,):
+            at_z = z + sign * distance
+
+            @pl.when((at_z >= 0) & (at_z < line))
+            def _():
+                origin = index(at_z, 1 - row, core)
+                arrived(origin, p)
+                send(TWIN, origin, p, tables[p].at[origin])
+
+    def from_twin(p):
+        for at_z in range(line):
+            for at_row in range(2):
+                arrived(index(at_z, at_row, 1 - core), p)
+
+    lane = lax.broadcasted_iota(jnp.int32, (width, 2 * width), 1)
+
+    def prepare():
+        for k in range(supernodes):
+            length = jnp.full(lane.shape, lengths[k], jnp.int32)
+            for p in range(poles):
+                for s in range(blocks):
+                    start = s // 2 * 2 * width
+                    strip = factor[k, p, :, start:start + 2 * width].astype(jnp.float32)
+                    half = jnp.full(lane.shape, lax.rem(pattern[k, s], 2), jnp.int32)
+                    swapped = jnp.concatenate([strip[:, width:], strip[:, :width]], axis=1)
+                    placed = jnp.where(half == s % 2, strip, swapped)
+                    keep = (lane // width == half) & (s < length)
+                    spread[k, p, :, s * 2 * width:(s + 1) * 2 * width] = jnp.where(
+                        keep, placed, 0.0
+                    ).astype(jnp.bfloat16)
+
+    wide = lax.broadcasted_iota(jnp.int32, (width, blocks * width), 1)
+    contract = (((1,), (1,)), ((), ()))
+
+    def compute(p):
+        for k in range(supernodes):
+            strips = [lax.div(pattern[k, s], 2) for s in range(blocks)]
+            picked = jnp.concatenate(
+                [
+                    jnp.concatenate([tables[p][pattern[k, r], strip] for strip in strips], axis=1)
+                    for r in range(blocks)
+                ],
+                axis=0,
+            )
+            product = lax.dot_general(spread[k, p], picked, contract, preferred_element_type=jnp.float32)
+            product = jnp.where(wide < jnp.full(wide.shape, lengths[k] * width, jnp.int32), product, 0.0)
+            rounded = product.astype(jnp.bfloat16)
+            held = rounded.astype(jnp.float32)
+            row_out[k, p] = (-held).astype(jnp.bfloat16)
+            term = lax.dot_general(factor[k, p], rounded, contract, preferred_element_type=jnp.float32)
+            columns = slice(p * width, (p + 1) * width)
+            diag_out[k, :, columns] = diag[k, :, columns] + term
+            total = weight[p] * held
+            if p > 0:
+                total = partial[k] + total
+            if p < poles - 1:
+                partial[k] = total
+            else:
+                density_out[k] = (-total).astype(jnp.bfloat16)
+
+    def stage(p, step):
+        if 1 <= step < line:
+            from_line(p, LEFT, step)
+            from_line(p, RIGHT, step)
+        if 1 <= step <= line:
+            from_across(p, step - 1)
+        if step == line + 1:
+            from_twin(p)
+            compute(p)
+
+    for p in range(poles):
+        own(p)
+    factor_in.wait()
+    diag_in.wait()
+    prepare()
+    for step in range(1, line + 2 + lag * (poles - 1)):
+        for p in range(poles):
+            stage(p, step - lag * p)
+
+    def left_device(way, origin, p):
+        remote(way, origin, p, tables[p].at[origin]).wait_send()
+
+    for p in range(poles):
+        for at_z in range(line):
+            origin = index(at_z, row, core)
+            pl.when(has[LEFT] & (at_z >= z))(functools.partial(left_device, LEFT, origin, p))
+            pl.when(has[RIGHT] & (at_z <= z))(functools.partial(left_device, RIGHT, origin, p))
+            left_device(ACROSS, origin, p)
+            for at_row in range(2):
+                left_device(TWIN, index(at_z, at_row, core), p)
+
+
+def gathered(ancestor_rows, factor_rows, pattern, lengths, diag_inverse, pole_weight):
+    supernodes, poles, width, span = factor_rows.shape
+    n = lax.axis_size("col")
+    blocks = pattern.shape[1]
+    smem = pl.BlockSpec(memory_space=pltpu.SMEM)
+    vmem = pl.BlockSpec(memory_space=pltpu.VMEM)
+    anywhere = pl.BlockSpec(memory_space=pl.ANY)
+    return pl.pallas_call(
+        functools.partial(gather_kernel, n // 4, 1),
+        out_shape=(
+            jax.ShapeDtypeStruct(factor_rows.shape, jnp.bfloat16),
+            jax.ShapeDtypeStruct(diag_inverse.shape, jnp.float32),
+            jax.ShapeDtypeStruct((supernodes, width, span), jnp.bfloat16),
+        ),
+        in_specs=[smem, smem, smem, vmem, anywhere, anywhere],
+        out_specs=(vmem, vmem, vmem),
+        scratch_shapes=[
+            pltpu.VMEM((n, ancestor_rows.shape[2] // (2 * width), width, 2 * width), jnp.bfloat16)
+            for _ in range(poles)
+        ]
+        + [
+            pltpu.VMEM(factor_rows.shape, jnp.bfloat16),
+            pltpu.VMEM(diag_inverse.shape, jnp.float32),
+            pltpu.VMEM((supernodes, poles, width, 2 * blocks * width), jnp.bfloat16),
+            pltpu.VMEM((supernodes, width, span), jnp.float32),
+            pltpu.SemaphoreType.DMA((4, n, poles)),
+            pltpu.SemaphoreType.DMA((n, poles)),
+            pltpu.SemaphoreType.DMA((2,)),
+        ],
+        compiler_params=pltpu.CompilerParams(
+            collective_id=0, has_side_effects=True, vmem_limit_bytes=VMEM_BYTES
+        ),
+    )(pattern, lengths, pole_weight, ancestor_rows, factor_rows, diag_inverse)
 
 
 def slot_layout(pattern, lengths, devices_total, capacity):
@@ -27,7 +244,7 @@
     return (live_slots, live_flat, slot_of_pair, source_pair // blocks, occupied)
 
 
-def shards(ancestor_rows, factor_rows, pattern, lengths, diag_inverse, pole_weight):
+def routed(ancestor_rows, factor_rows, pattern, lengths, diag_inverse, pole_weight):
     supernodes, pole_count, block_width, row_span = factor_rows.shape
     blocks = pattern.shape[1]
     devices_total = lax.axis_size("col")
@@ -79,6 +296,13 @@
     return (inverse_row, inverse_diag, density.astype(jnp.bfloat16))
 
 
+def shards(ancestor_rows, *others):
+    n = lax.axis_size("col")
+    if n % 4 == 0 and n * ancestor_rows.size * ancestor_rows.dtype.itemsize <= TABLE_BYTES:
+        return gathered(ancestor_rows, *others)
+    return routed(ancestor_rows, *others)
+
+
 def solution(mesh):
     placed = (
         P("kpt", "col", None),

time: 99.3 us -> 41.3 us (0.42)
  Pallas kernels: 0 us -> 34.8 us
  waiting for transfers between devices: 34.5 us -> 0 us
  local copies, waits for them, and re-layouts: 30 us -> 5.68 us
  starting transfers between devices: 23.1 us -> 0 us
  other arithmetic: 7.35 us -> 0 us
  matrix products: 2.51 us -> 0 us
    pallas_call x0 -> x1, Pallas kernels: none -> 34.8 us  [gathered(): pl.pallas_call(functools.partial(gather_kernel, n // 4, 1), out_shape=(ja...]
    all_to_all x3 -> x0, waiting for transfers between devices: 34.5 us -> none  [the longest x1 19 us: shards(): lax.all_to_all(outgoing, 'col', split_axis=0, concat_axis=0, tiled=True)]
    gather x6 -> x0, local copies, waits for them, and re-layouts: 23.6 us -> none  [the longest x3 21.7 us: shards(): gathered = jnp.take(table, indices, axis=2)]
    all_to_all x3 -> x0, starting transfers between devices: 23.1 us -> none  [the longest x1 10.8 us: shards(): lax.all_to_all(rounded, 'col', split_axis=0, concat_axis=0, tiled=True)]
    unnamed x7 -> x14, local copies, waits for them, and re-layouts: 0.78 us -> 5.68 us
    reshape x8 -> x0, local copies, waits for them, and re-layouts: 2.92 us -> none  [the longest x1 1.14 us: shards(): products.astype(jnp.bfloat16)]
    dot_general x2 -> x0, matrix products: 2.51 us -> none  [the longest x1 2.28 us: shards(): jnp.einsum('ncpix,pjncx->ncipj', factor_part, gathered, preferred_element...]
    select_n x6 -> x0, other arithmetic: 2.31 us -> none  [the longest x1 1.55 us: shards(): outgoing = jnp.take(masked_factor, source_super, axis=0)]
  transfers between devices with their start and end apart: 3 -> 0, of which waited for: 3 -> 0; matrix products, arithmetic and copies ran while one was open for 27% -> 0% of each run, Pallas kernels for 0% -> 0%
where the time goes in v1:
time: 41.3 us; the launch traced here: 41.1 us
  Pallas kernels  34.8 us (84%)
  local copies, waits for them, and re-layouts  5.68 us (14%)
  between operations  0.66 us (2%)
    pallas_call x1, Pallas kernels, gathered(): pl.pallas_call(functools.partial(gather_kernel, n // 4, 1), out_shape=(ja...  34.8 us
    unnamed x14, local copies, waits for them, and re-layouts  5.68 us

profile of v1, /device:TPU:1, one launch (start us, length us, event | category | flops | bytes accessed | tf_op | source)
XLA Modules:
  0.0 41.1 jit_solution(15970744691575225320)
XLA Ops:
  0.6 0.0 copy-start.4
  0.6 0.0 copy-start.3
  0.7 0.8 %copy.9.pattern = s32[5,4]{1,0:T(8,128)S(1)} copy(s32[5,4]{0,1:T(4,128)} %param.8) | data formatting | bytes 160 | tf_op args[2]
  1.4 0.0 copy-done.4
  1.4 0.0 copy-done.3
  1.4 0.0 copy-start
  1.4 1.0 %copy-done = bf16[5,2,64,256]{3,2,1,0:T(8,128)(2,1)S(1)} copy-done((bf16[5,2,64,256]{3,2,1,0:T(8,128)(2,1)S(1)}, bf16[5,2,64,256]{3,2,1,0:T(8,128)(2,1)}, u32[]{:S(2)}) %copy-start) | copy-done | bytes 327704
  2.4 0.0 copy-start.1
  2.4 0.9 %copy-done.1 = bf16[2,64,1024]{2,1,0:T(8,128)(2,1)S(1)} copy-done((bf16[2,64,1024]{2,1,0:T(8,128)(2,1)S(1)}, bf16[2,64,1024]{2,1,0:T(8,128)(2,1)}, u32[]{:S(2)}) %copy-start.1) | copy-done | bytes 262168
  3.4 0.0 copy-start.2
  3.4 0.9 %copy-done.2 = f32[5,64,128]{2,1,0:T(8,128)S(1)} copy-done((f32[5,64,128]{2,1,0:T(8,128)S(1)}, f32[5,64,128]{2,1,0:T(8,128)}, u32[]{:S(2)}) %copy-start.2) | copy-done | bytes 163864
  4.3 34.8 %shard_map.85 = (bf16[5,2,64,256]{3,2,1,0:T(8,128)(2,1)S(1)}, f32[5,64,128]{2,1,0:T(8,128)S(1)}, bf16[5,64,256]{2,1,0:T(8,128)(2,1)S(1)}) custom-call(s32[5,4]{1,0:T(8,128)S(1)} %copy.9.pattern, s32[5]{0:T(128)S(1)} %copy-done.3, f32[2]{0:T(128)S(1)} %copy-done.4, bf16[2,64,1024]{2,1,0:T(8,128)(2,1)S(1)} %copy-done.1, bf16[5,2,64,256]{3,2,1,0:T(8,128)(2,1)S(1)} %copy-done, ...), custom_call_target="tpu_custom_call" | custom-call | tf_op jit(solution)/shard_map/pallas_call | solution.py:198
  39.1 0.7 %copy.13 = bf16[5,2,64,256]{3,2,1,0:T(8,128)(2,1)} copy(bf16[5,2,64,256]{3,2,1,0:T(8,128)(2,1)S(1)} %get-tuple-element.6) | data formatting | bytes 655360
  39.8 0.7 %copy.14 = f32[5,64,128]{2,1,0:T(8,128)} copy(f32[5,64,128]{2,1,0:T(8,128)S(1)} %get-tuple-element.7) | data formatting | bytes 327680
  40.5 0.7 %copy.15 = bf16[5,64,256]{2,1,0:T(8,128)(2,1)} copy(bf16[5,64,256]{2,1,0:T(8,128)(2,1)S(1)} %get-tuple-element.8) | data formatting | bytes 327680
Async XLA Ops:
  0.6 0.8 %copy-start.4 = (f32[2]{0:T(128)S(1)}, f32[2]{0:T(128)}, u32[]{:S(2)}) copy-start(f32[2]{0:T(128)} %weight.1) | copy-start | bytes 28
  0.6 0.8 %copy-start.3 = (s32[5]{0:T(128)S(1)}, s32[5]{0:T(128)}, u32[]{:S(2)}) copy-start(s32[5]{0:T(128)} %lengths.1) | copy-start | bytes 64
  1.4 1.0 %copy-start = (bf16[5,2,64,256]{3,2,1,0:T(8,128)(2,1)S(1)}, bf16[5,2,64,256]{3,2,1,0:T(8,128)(2,1)}, u32[]{:S(2)}) copy-start(bf16[5,2,64,256]{3,2,1,0:T(8,128)(2,1)} %factor_hbm.1) | copy-start | bytes 983044
  2.4 0.9 %copy-start.1 = (bf16[2,64,1024]{2,1,0:T(8,128)(2,1)S(1)}, bf16[2,64,1024]{2,1,0:T(8,128)(2,1)}, u32[]{:S(2)}) copy-start(bf16[2,64,1024]{2,1,0:T(8,128)(2,1)} %anc.1) | copy-start | bytes 786436
  3.4 0.9 %copy-start.2 = (f32[5,64,128]{2,1,0:T(8,128)S(1)}, f32[5,64,128]{2,1,0:T(8,128)}, u32[]{:S(2)}) copy-start(f32[5,64,128]{2,1,0:T(8,128)} %diag_hbm.1) | copy-start | bytes 491524

commit v2 on v1

--- a/solution.py
+++ b/solution.py
@@ -10,21 +10,21 @@
 CAP = 2
 MESH = pl.DeviceIdType.MESH
 TABLE_BYTES = 16 * 2**20
-VMEM_BYTES = 32 * 2**20
+VMEM_BYTES = 60 * 2**20
 LEFT, RIGHT, ACROSS, TWIN = range(4)
 
 
 def gather_kernel(
-    line, lag,
-    pattern, lengths, weight, anc, factor_hbm, diag_hbm,
+    line,
+    pattern, lengths, weight, anc_hbm, factor_hbm, diag_hbm,
     row_out, diag_out, density_out,
     *scratch,
 ):
-    poles, width, span = anc.shape
+    poles, width, span = anc_hbm.shape
     tables = scratch[:poles]
-    factor, diag, spread, partial, send_sem, recv_sem, local_sem = scratch[poles:]
+    anc, factor, diag, spread, partial, send_sem, recv_sem, local_sem = scratch[poles:]
     supernodes = factor.shape[0]
-    blocks = pattern.shape[1]
+    blocks = pattern.shape[0]
     me = lax.axis_index("col")
     core, row, z = me % 2, (me // 2) % 2, me // 4
 
@@ -41,11 +41,10 @@
 
     factor_in = pltpu.make_async_copy(factor_hbm, factor, local_sem.at[0])
     diag_in = pltpu.make_async_copy(diag_hbm, diag, local_sem.at[1])
+    anc_in = pltpu.make_async_copy(anc_hbm, anc, local_sem.at[2])
+    anc_in.start()
     factor_in.start()
     diag_in.start()
-    for p in range(poles):
-        for strip in range(span // (2 * width)):
-            tables[p][me, strip] = anc[p, :, strip * 2 * width:(strip + 1) * 2 * width]
 
     barrier = pltpu.get_barrier_semaphore()
 
@@ -56,6 +55,10 @@
     greet(ACROSS)
     for way in (LEFT, RIGHT):
         pl.when(has[way])(functools.partial(greet, way))
+    anc_in.wait()
+    for p in range(poles):
+        for strip in range(span // (2 * width)):
+            tables[p][me, strip] = anc[p, :, strip * 2 * width:(strip + 1) * 2 * width]
     pl.semaphore_wait(barrier, 2 + has[LEFT].astype(jnp.int32) + has[RIGHT].astype(jnp.int32))
 
     def remote(way, origin, p, source):
@@ -81,6 +84,9 @@
         send(ACROSS, me, p, block)
         send(TWIN, me, p, block)
 
+    def by_line(at_z, p):
+        return ((at_z == 0) | (at_z == line - 1)) & (p == poles - 1)
+
     def from_line(p, side, distance):
         at_z = z - distance if side == LEFT else z + distance
         inside = at_z >= 0 if side == LEFT else at_z < line
@@ -92,18 +98,39 @@
             arrived(origin, p)
             block = tables[p].at[origin]
             pl.when(has[onward])(functools.partial(send, onward, origin, p, block))
-            send(ACROSS, origin, p, block)
+            pl.when(jnp.logical_not(by_line(at_z, p)))(functools.partial(send, ACROSS, origin, p, block))
+            send(TWIN, origin, p, block)
+
+    def from_other_line(p, side, distance):
+        at_z = z - distance if side == LEFT else z + distance
+        inside = at_z >= 0 if side == LEFT else at_z < line
+        onward = RIGHT if side == LEFT else LEFT
+
+        @pl.when(inside & by_line(at_z, p))
+        def _():
+            origin = index(at_z, 1 - row, core)
+            arrived(origin, p)
+            block = tables[p].at[origin]
+            pl.when(has[onward])(functools.partial(send, onward, origin, p, block))
             send(TWIN, origin, p, block)
 
     def from_across(p, distance):
         for sign in (-1, 1) if distance else (1,):
             at_z = z + sign * distance
 
-            @pl.when((at_z >= 0) & (at_z < line))
+            crosses = (at_z >= 0) & (at_z < line)
+            if distance:
+                crosses = crosses & jnp.logical_not(by_line(at_z, p))
+
+            @pl.when(crosses)
             def _():
                 origin = index(at_z, 1 - row, core)
                 arrived(origin, p)
-                send(TWIN, origin, p, tables[p].at[origin])
+                block = tables[p].at[origin]
+                if not distance:
+                    for way in (LEFT, RIGHT):
+                        pl.when(has[way] & by_line(z, p))(functools.partial(send, way, origin, p, block))
+                send(TWIN, origin, p, block)
 
     def from_twin(p):
         for at_z in range(line):
@@ -119,7 +146,7 @@
                 for s in range(blocks):
                     start = s // 2 * 2 * width
                     strip = factor[k, p, :, start:start + 2 * width].astype(jnp.float32)
-                    half = jnp.full(lane.shape, lax.rem(pattern[k, s], 2), jnp.int32)
+                    half = jnp.full(lane.shape, lax.rem(pattern[s, k], 2), jnp.int32)
                     swapped = jnp.concatenate([strip[:, width:], strip[:, :width]], axis=1)
                     placed = jnp.where(half == s % 2, strip, swapped)
                     keep = (lane // width == half) & (s < length)
@@ -131,49 +158,56 @@
     contract = (((1,), (1,)), ((), ()))
 
     def compute(p):
-        for k in range(supernodes):
-            strips = [lax.div(pattern[k, s], 2) for s in range(blocks)]
+        columns = slice(p * width, (p + 1) * width)
+        products, terms = [], []
+        for k in range(supernodes):
+            strips = [lax.div(pattern[s, k], 2) for s in range(blocks)]
             picked = jnp.concatenate(
                 [
-                    jnp.concatenate([tables[p][pattern[k, r], strip] for strip in strips], axis=1)
+                    jnp.concatenate([tables[p][pattern[r, k], strip] for strip in strips], axis=1)
                     for r in range(blocks)
                 ],
                 axis=0,
             )
             product = lax.dot_general(spread[k, p], picked, contract, preferred_element_type=jnp.float32)
-            product = jnp.where(wide < jnp.full(wide.shape, lengths[k] * width, jnp.int32), product, 0.0)
-            rounded = product.astype(jnp.bfloat16)
-            held = rounded.astype(jnp.float32)
-            row_out[k, p] = (-held).astype(jnp.bfloat16)
-            term = lax.dot_general(factor[k, p], rounded, contract, preferred_element_type=jnp.float32)
-            columns = slice(p * width, (p + 1) * width)
-            diag_out[k, :, columns] = diag[k, :, columns] + term
-            total = weight[p] * held
+            live = wide < jnp.full(wide.shape, lengths[k] * width, jnp.int32)
+            products.append(jnp.where(live, product, 0.0).astype(jnp.bfloat16))
+        for k in range(supernodes):
+            terms.append(
+                lax.dot_general(factor[k, p], products[k], contract, preferred_element_type=jnp.float32)
+            )
+        for k in range(supernodes):
+            row_out[k, p] = -products[k]
+            total = weight[p] * products[k].astype(jnp.float32)
             if p > 0:
                 total = partial[k] + total
             if p < poles - 1:
                 partial[k] = total
             else:
                 density_out[k] = (-total).astype(jnp.bfloat16)
-
-    def stage(p, step):
-        if 1 <= step < line:
-            from_line(p, LEFT, step)
-            from_line(p, RIGHT, step)
-        if 1 <= step <= line:
-            from_across(p, step - 1)
-        if step == line + 1:
-            from_twin(p)
-            compute(p)
+        for k in range(supernodes):
+            diag_out[k, :, columns] = diag[k, :, columns] + terms[k]
 
     for p in range(poles):
         own(p)
     factor_in.wait()
     diag_in.wait()
     prepare()
-    for step in range(1, line + 2 + lag * (poles - 1)):
-        for p in range(poles):
-            stage(p, step - lag * p)
+    last = poles - 1
+    steps = []
+    for p in range(poles):
+        for distance in range(1, line):
+            for side in (LEFT, RIGHT):
+                steps.append((poles * (distance - 1) + p, 0, functools.partial(from_line, p, side, distance)))
+                if p == last:
+                    steps.append((poles * distance, -1, functools.partial(from_other_line, p, side, distance)))
+        for distance in range(line):
+            steps.append((poles * distance + p, 1, functools.partial(from_across, p, distance)))
+    for _, _, step in sorted(steps, key=lambda entry: entry[:2]):
+        step()
+    for p in range(poles):
+        from_twin(p)
+        compute(p)
 
     def left_device(way, origin, p):
         remote(way, origin, p, tables[p].at[origin]).wait_send()
@@ -183,9 +217,29 @@
             origin = index(at_z, row, core)
             pl.when(has[LEFT] & (at_z >= z))(functools.partial(left_device, LEFT, origin, p))
             pl.when(has[RIGHT] & (at_z <= z))(functools.partial(left_device, RIGHT, origin, p))
-            left_device(ACROSS, origin, p)
+            pl.when(jnp.logical_not(by_line(at_z, p)) | (z == at_z))(functools.partial(left_device, ACROSS, origin, p))
+            other = index(at_z, 1 - row, core)
+            pl.when(has[LEFT] & (at_z >= z) & by_line(at_z, p))(functools.partial(left_device, LEFT, other, p))
+            pl.when(has[RIGHT] & (at_z <= z) & by_line(at_z, p))(functools.partial(left_device, RIGHT, other, p))
             for at_row in range(2):
                 left_device(TWIN, index(at_z, at_row, core), p)
+
+
+def write_kernel(*refs):
+    count = len(refs) // 3
+    sources, targets, held, sem = refs[:count], refs[count:2 * count], refs[2 * count:3 * count], refs[-1]
+    copies = []
+    for i in range(count):
+        for k in range(sources[i].shape[0]):
+            loads = pltpu.make_async_copy(sources[i].at[k], held[i].at[k], sem.at[i, k, 0])
+            stores = pltpu.make_async_copy(held[i].at[k], targets[i].at[k], sem.at[i, k, 1])
+            copies.append((loads, stores))
+            loads.start()
+    for loads, stores in copies:
+        loads.wait()
+        stores.start()
+    for _, stores in copies:
+        stores.wait()
 
 
 def gathered(ancestor_rows, factor_rows, pattern, lengths, diag_inverse, pole_weight):
@@ -195,32 +249,41 @@
     smem = pl.BlockSpec(memory_space=pltpu.SMEM)
     vmem = pl.BlockSpec(memory_space=pltpu.VMEM)
     anywhere = pl.BlockSpec(memory_space=pl.ANY)
-    return pl.pallas_call(
-        functools.partial(gather_kernel, n // 4, 1),
+    results = pl.pallas_call(
+        functools.partial(gather_kernel, n // 4),
         out_shape=(
             jax.ShapeDtypeStruct(factor_rows.shape, jnp.bfloat16),
             jax.ShapeDtypeStruct(diag_inverse.shape, jnp.float32),
             jax.ShapeDtypeStruct((supernodes, width, span), jnp.bfloat16),
         ),
-        in_specs=[smem, smem, smem, vmem, anywhere, anywhere],
+        in_specs=[smem, smem, smem, anywhere, anywhere, anywhere],
         out_specs=(vmem, vmem, vmem),
         scratch_shapes=[
             pltpu.VMEM((n, ancestor_rows.shape[2] // (2 * width), width, 2 * width), jnp.bfloat16)
             for _ in range(poles)
         ]
         + [
+            pltpu.VMEM(ancestor_rows.shape, jnp.bfloat16),
             pltpu.VMEM(factor_rows.shape, jnp.bfloat16),
             pltpu.VMEM(diag_inverse.shape, jnp.float32),
             pltpu.VMEM((supernodes, poles, width, 2 * blocks * width), jnp.bfloat16),
             pltpu.VMEM((supernodes, width, span), jnp.float32),
             pltpu.SemaphoreType.DMA((4, n, poles)),
             pltpu.SemaphoreType.DMA((n, poles)),
-            pltpu.SemaphoreType.DMA((2,)),
+            pltpu.SemaphoreType.DMA((3,)),
         ],
         compiler_params=pltpu.CompilerParams(
             collective_id=0, has_side_effects=True, vmem_limit_bytes=VMEM_BYTES
         ),
-    )(pattern, lengths, pole_weight, ancestor_rows, factor_rows, diag_inverse)
+    )(pattern.T, lengths, pole_weight, ancestor_rows, factor_rows, diag_inverse)
+    return pl.pallas_call(
+        write_kernel,
+        out_shape=tuple(jax.ShapeDtypeStruct(x.shape, x.dtype) for x in results),
+        in_specs=[anywhere] * 3,
+        out_specs=(anywhere,) * 3,
+        scratch_shapes=[pltpu.VMEM(x.shape, x.dtype) for x in results]
+        + [pltpu.SemaphoreType.DMA((3, supernodes, 2))],
+    )(*results)
 
 
 def slot_layout(pattern, lengths, devices_total, capacity):

time: 41.3 us -> 33.5 us (0.81)
  local copies, waits for them, and re-layouts: 5.68 us -> 0 us
  Pallas kernels: 34.8 us -> 32.6 us
    unnamed x14 -> x0, local copies, waits for them, and re-layouts: 5.68 us -> none
    pallas_call x1 -> x2, Pallas kernels: 34.8 us -> 32.6 us  [the longest x1 30.7 us: gathered(): pl.pallas_call(functools.partial(gather_kernel, n // 4), out_shape=(jax.S...]
where the time goes in v2:
time: 33.5 us; the launch traced here: 33.3 us
  Pallas kernels  32.6 us (97%)
  between operations  0.64 us (2%)
    pallas_call x1, Pallas kernels, gathered(): pl.pallas_call(functools.partial(gather_kernel, n // 4), out_shape=(jax.S...  30.7 us
    pallas_call x1, Pallas kernels, gathered(): pl.pallas_call(write_kernel, out_shape=tuple((jax.ShapeDtypeStruct(x.shap...  1.96 us

profile of v2, /device:TPU:1, one launch (start us, length us, event | category | flops | bytes accessed | tf_op | source)
XLA Modules:
  0.0 33.3 jit_solution(2620698680311664966)
XLA Ops:
  0.6 30.7 %shard_map.85 = (bf16[5,2,64,256]{3,2,1,0:T(8,128)(2,1)}, f32[5,64,128]{2,1,0:T(8,128)}, bf16[5,64,256]{2,1,0:T(8,128)(2,1)}) custom-call(s32[4,5]{1,0:T(4,128)} %bitcast.1, s32[5]{0:T(128)} %lengths.1, f32[2]{0:T(128)} %weight.1, bf16[2,64,1024]{2,1,0:T(8,128)(2,1)} %anc_hbm.1, bf16[5,2,64,256]{3,2,1,0:T(8,128)(2,1)} %factor_hbm.1, f32[5,64,128]{2,1,0:T(8,128)} %diag_hbm.1), custom_call_target="tpu_custom_call" | custom-call | tf_op jit(solution)/shard_map/pallas_call | solution.py:252
  31.3 2.0 %shard_map.86 = (bf16[5,2,64,256]{3,2,1,0:T(8,128)(2,1)}, f32[5,64,128]{2,1,0:T(8,128)}, bf16[5,64,256]{2,1,0:T(8,128)(2,1)}) custom-call(bf16[5,2,64,256]{3,2,1,0:T(8,128)(2,1)} %get-tuple-element.6.refs_0_, f32[5,64,128]{2,1,0:T(8,128)} %get-tuple-element.7.refs_1_, bf16[5,64,256]{2,1,0:T(8,128)(2,1)} %get-tuple-element.8.refs_2_), custom_call_target="tpu_custom_call" | custom-call | tf_op jit(solution)/shard_map/pallas_call | solution.py:279

commit v3 on v2

--- a/solution.py
+++ b/solution.py
@@ -16,13 +16,14 @@
 
 def gather_kernel(
     line,
-    pattern, lengths, weight, anc_hbm, factor_hbm, diag_hbm,
+    pattern_hbm, lengths_hbm, weight_hbm, anc_hbm, factor_hbm, diag_hbm,
     row_out, diag_out, density_out,
     *scratch,
 ):
     poles, width, span = anc_hbm.shape
     tables = scratch[:poles]
-    anc, factor, diag, spread, partial, send_sem, recv_sem, local_sem = scratch[poles:]
+    pattern, lengths, weight, anc, factor, diag, spread, partial = scratch[poles:poles + 8]
+    send_sem, recv_sem, local_sem = scratch[poles + 8:]
     supernodes = factor.shape[0]
     blocks = pattern.shape[0]
     me = lax.axis_index("col")
@@ -39,12 +40,13 @@
     }
     has = {LEFT: z > 0, RIGHT: z < line - 1}
 
-    factor_in = pltpu.make_async_copy(factor_hbm, factor, local_sem.at[0])
-    diag_in = pltpu.make_async_copy(diag_hbm, diag, local_sem.at[1])
-    anc_in = pltpu.make_async_copy(anc_hbm, anc, local_sem.at[2])
-    anc_in.start()
-    factor_in.start()
-    diag_in.start()
+    pairs = (
+        (anc_hbm, anc), (pattern_hbm, pattern), (lengths_hbm, lengths), (weight_hbm, weight),
+        (factor_hbm, factor), (diag_hbm, diag),
+    )
+    incoming = [pltpu.make_async_copy(a, b, local_sem.at[i]) for i, (a, b) in enumerate(pairs)]
+    for copy in incoming:
+        copy.start()
 
     barrier = pltpu.get_barrier_semaphore()
 
@@ -55,7 +57,7 @@
     greet(ACROSS)
     for way in (LEFT, RIGHT):
         pl.when(has[way])(functools.partial(greet, way))
-    anc_in.wait()
+    incoming[0].wait()
     for p in range(poles):
         for strip in range(span // (2 * width)):
             tables[p][me, strip] = anc[p, :, strip * 2 * width:(strip + 1) * 2 * width]
@@ -154,6 +156,7 @@
                         keep, placed, 0.0
                     ).astype(jnp.bfloat16)
 
+    last = poles - 1
     wide = lax.broadcasted_iota(jnp.int32, (width, blocks * width), 1)
     contract = (((1,), (1,)), ((), ()))
 
@@ -190,10 +193,9 @@
 
     for p in range(poles):
         own(p)
-    factor_in.wait()
-    diag_in.wait()
+    for copy in incoming[1:]:
+        copy.wait()
     prepare()
-    last = poles - 1
     steps = []
     for p in range(poles):
         for distance in range(1, line):
@@ -226,43 +228,38 @@
 
 
 def write_kernel(*refs):
-    count = len(refs) // 3
-    sources, targets, held, sem = refs[:count], refs[count:2 * count], refs[2 * count:3 * count], refs[-1]
-    copies = []
-    for i in range(count):
-        for k in range(sources[i].shape[0]):
-            loads = pltpu.make_async_copy(sources[i].at[k], held[i].at[k], sem.at[i, k, 0])
-            stores = pltpu.make_async_copy(held[i].at[k], targets[i].at[k], sem.at[i, k, 1])
-            copies.append((loads, stores))
-            loads.start()
-    for loads, stores in copies:
-        loads.wait()
-        stores.start()
-    for _, stores in copies:
-        stores.wait()
+    count = len(refs) // 2
+    sources, targets, sem = refs[:count], refs[count:2 * count], refs[-1]
+    copies = [pltpu.make_async_copy(a, b, sem.at[i]) for i, (a, b) in enumerate(zip(sources, targets))]
+    for copy in copies:
+        copy.start()
+    for copy in copies:
+        copy.wait()
 
 
 def gathered(ancestor_rows, factor_rows, pattern, lengths, diag_inverse, pole_weight):
     supernodes, poles, width, span = factor_rows.shape
     n = lax.axis_size("col")
     blocks = pattern.shape[1]
-    smem = pl.BlockSpec(memory_space=pltpu.SMEM)
+    anywhere = pl.BlockSpec(memory_space=pl.ANY)
     vmem = pl.BlockSpec(memory_space=pltpu.VMEM)
-    anywhere = pl.BlockSpec(memory_space=pl.ANY)
     results = pl.pallas_call(
         functools.partial(gather_kernel, n // 4),
         out_shape=(
-            jax.ShapeDtypeStruct(factor_rows.shape, jnp.bfloat16),
-            jax.ShapeDtypeStruct(diag_inverse.shape, jnp.float32),
-            jax.ShapeDtypeStruct((supernodes, width, span), jnp.bfloat16),
+            pltpu.VMEM(factor_rows.shape, jnp.bfloat16),
+            pltpu.VMEM(diag_inverse.shape, jnp.float32),
+            pltpu.VMEM((supernodes, width, span), jnp.bfloat16),
         ),
-        in_specs=[smem, smem, smem, anywhere, anywhere, anywhere],
-        out_specs=(vmem, vmem, vmem),
+        in_specs=[anywhere] * 6,
+        out_specs=(vmem,) * 3,
         scratch_shapes=[
             pltpu.VMEM((n, ancestor_rows.shape[2] // (2 * width), width, 2 * width), jnp.bfloat16)
             for _ in range(poles)
         ]
         + [
+            pltpu.SMEM((blocks, supernodes), jnp.int32),
+            pltpu.SMEM(lengths.shape, jnp.int32),
+            pltpu.SMEM(pole_weight.shape, jnp.float32),
             pltpu.VMEM(ancestor_rows.shape, jnp.bfloat16),
             pltpu.VMEM(factor_rows.shape, jnp.bfloat16),
             pltpu.VMEM(diag_inverse.shape, jnp.float32),
@@ -270,19 +267,19 @@
             pltpu.VMEM((supernodes, width, span), jnp.float32),
             pltpu.SemaphoreType.DMA((4, n, poles)),
             pltpu.SemaphoreType.DMA((n, poles)),
-            pltpu.SemaphoreType.DMA((3,)),
+            pltpu.SemaphoreType.DMA((6,)),
         ],
         compiler_params=pltpu.CompilerParams(
             collective_id=0, has_side_effects=True, vmem_limit_bytes=VMEM_BYTES
         ),
     )(pattern.T, lengths, pole_weight, ancestor_rows, factor_rows, diag_inverse)
+    results = [pltpu.with_memory_space_constraint(x, pltpu.VMEM) for x in results]
     return pl.pallas_call(
         write_kernel,
         out_shape=tuple(jax.ShapeDtypeStruct(x.shape, x.dtype) for x in results),
-        in_specs=[anywhere] * 3,
+        in_specs=[vmem] * 3,
         out_specs=(anywhere,) * 3,
-        scratch_shapes=[pltpu.VMEM(x.shape, x.dtype) for x in results]
-        + [pltpu.SemaphoreType.DMA((3, supernodes, 2))],
+        scratch_shapes=[pltpu.SemaphoreType.DMA((3,))],
     )(*results)
 
 

time: 33.5 us -> 30.8 us (0.919)
  Pallas kernels: 32.6 us -> 30 us
    pallas_call x1, Pallas kernels: 30.7 us -> 29.2 us  [gathered(): pl.pallas_call(functools.partial(gather_kernel, n // 4), out_shape=(pltpu...]
    pallas_call x1, Pallas kernels: 1.96 us -> 0.86 us  [gathered(): pl.pallas_call(write_kernel, out_shape=tuple((jax.ShapeDtypeStruct(x.shap...]
where the time goes in v3:
time: 30.8 us; the launch traced here: 30.7 us
  Pallas kernels  30 us (97%)
  between operations  0.64 us (2%)
    pallas_call x1, Pallas kernels, gathered(): pl.pallas_call(functools.partial(gather_kernel, n // 4), out_shape=(pltpu...  29.2 us
    pallas_call x1, Pallas kernels, gathered(): pl.pallas_call(write_kernel, out_shape=tuple((jax.ShapeDtypeStruct(x.shap...  0.86 us

profile of v3, /device:TPU:1, one launch (start us, length us, event | category | flops | bytes accessed | tf_op | source)
XLA Modules:
  0.0 30.7 jit_solution(9259354799150640550)
XLA Ops:
  0.6 29.2 %shard_map.85 = (bf16[5,2,64,256]{3,2,1,0:T(8,128)(2,1)S(1)}, f32[5,64,128]{2,1,0:T(8,128)S(1)}, bf16[5,64,256]{2,1,0:T(8,128)(2,1)S(1)}) custom-call(s32[4,5]{1,0:T(4,128)} %bitcast.1, s32[5]{0:T(128)} %lengths_hbm.1, f32[2]{0:T(128)} %weight_hbm.1, bf16[2,64,1024]{2,1,0:T(8,128)(2,1)} %anc_hbm.1, bf16[5,2,64,256]{3,2,1,0:T(8,128)(2,1)} %factor_hbm.1, ...), custom_call_target="tpu_custom_call" | custom-call | tf_op jit(solution)/shard_map/pallas_call | solution.py:246
  29.8 0.9 %shard_map.86 = (bf16[5,2,64,256]{3,2,1,0:T(8,128)(2,1)}, f32[5,64,128]{2,1,0:T(8,128)}, bf16[5,64,256]{2,1,0:T(8,128)(2,1)}) custom-call(bf16[5,2,64,256]{3,2,1,0:T(8,128)(2,1)S(1)} %get-tuple-element.6.refs_0_, f32[5,64,128]{2,1,0:T(8,128)S(1)} %get-tuple-element.7.refs_1_, bf16[5,64,256]{2,1,0:T(8,128)(2,1)S(1)} %get-tuple-element.8.refs_2_), custom_call_target="tpu_custom_call" | custom-call | tf_op jit(solution)/shard_map/pallas_call | solution.py:277

commit v4 on v3

--- a/solution.py
+++ b/solution.py
@@ -45,8 +45,7 @@
         (factor_hbm, factor), (diag_hbm, diag),
     )
     incoming = [pltpu.make_async_copy(a, b, local_sem.at[i]) for i, (a, b) in enumerate(pairs)]
-    for copy in incoming:
-        copy.start()
+    incoming[0].start()
 
     barrier = pltpu.get_barrier_semaphore()
 
@@ -57,10 +56,15 @@
     greet(ACROSS)
     for way in (LEFT, RIGHT):
         pl.when(has[way])(functools.partial(greet, way))
-    incoming[0].wait()
-    for p in range(poles):
+    for copy in incoming[1:]:
+        copy.start()
+
+    def lay_out(p):
         for strip in range(span // (2 * width)):
             tables[p][me, strip] = anc[p, :, strip * 2 * width:(strip + 1) * 2 * width]
+
+    incoming[0].wait()
+    lay_out(0)
     pl.semaphore_wait(barrier, 2 + has[LEFT].astype(jnp.int32) + has[RIGHT].astype(jnp.int32))
 
     def remote(way, origin, p, source):
@@ -191,11 +195,12 @@
         for k in range(supernodes):
             diag_out[k, :, columns] = diag[k, :, columns] + terms[k]
 
-    for p in range(poles):
+    own(0)
+    for p in range(1, poles):
+        lay_out(p)
         own(p)
     for copy in incoming[1:]:
         copy.wait()
-    prepare()
     steps = []
     for p in range(poles):
         for distance in range(1, line):
@@ -205,6 +210,7 @@
                     steps.append((poles * distance, -1, functools.partial(from_other_line, p, side, distance)))
         for distance in range(line):
             steps.append((poles * distance + p, 1, functools.partial(from_across, p, distance)))
+    steps.append((1, 5, prepare))
     for _, _, step in sorted(steps, key=lambda entry: entry[:2]):
         step()
     for p in range(poles):

time: 30.8 us -> 30.8 us (level)
  no operation moved by 1% of the time
where the time goes in v4:
time: 30.8 us; the launch traced here: 30.7 us
  Pallas kernels  30 us (97%)
  between operations  0.64 us (2%)
    pallas_call x1, Pallas kernels, gathered(): pl.pallas_call(functools.partial(gather_kernel, n // 4), out_shape=(pltpu...  29.2 us
    pallas_call x1, Pallas kernels, gathered(): pl.pallas_call(write_kernel, out_shape=tuple((jax.ShapeDtypeStruct(x.shap...  0.86 us

profile of v4, /device:TPU:1, one launch (start us, length us, event | category | flops | bytes accessed | tf_op | source)
XLA Modules:
  0.0 30.7 jit_solution(13459721891921600345)
XLA Ops:
  0.6 29.2 %shard_map.85 = (bf16[5,2,64,256]{3,2,1,0:T(8,128)(2,1)S(1)}, f32[5,64,128]{2,1,0:T(8,128)S(1)}, bf16[5,64,256]{2,1,0:T(8,128)(2,1)S(1)}) custom-call(s32[4,5]{1,0:T(4,128)} %bitcast.1, s32[5]{0:T(128)} %lengths_hbm.1, f32[2]{0:T(128)} %weight_hbm.1, bf16[2,64,1024]{2,1,0:T(8,128)(2,1)} %anc_hbm.1, bf16[5,2,64,256]{3,2,1,0:T(8,128)(2,1)} %factor_hbm.1, ...), custom_call_target="tpu_custom_call" | custom-call | tf_op jit(solution)/shard_map/pallas_call | solution.py:252
  29.8 0.9 %shard_map.86 = (bf16[5,2,64,256]{3,2,1,0:T(8,128)(2,1)}, f32[5,64,128]{2,1,0:T(8,128)}, bf16[5,64,256]{2,1,0:T(8,128)(2,1)}) custom-call(bf16[5,2,64,256]{3,2,1,0:T(8,128)(2,1)S(1)} %get-tuple-element.6.refs_0_, f32[5,64,128]{2,1,0:T(8,128)S(1)} %get-tuple-element.7.refs_1_, bf16[5,64,256]{2,1,0:T(8,128)(2,1)S(1)} %get-tuple-element.8.refs_2_), custom_call_target="tpu_custom_call" | custom-call | tf_op jit(solution)/shard_map/pallas_call | solution.py:283
